TPU v7x, 128 devices: a whole 4x4x4 slice. The times are simulated.
128 devices in a mesh: row: 16 (over y, z), col: 8 (over x, core).
Axes of the slice: x: 4, y: 4, z: 4, core: 2. Of those that a mesh axis runs over, the one named last changes fastest.
Arguments:
- anchor_mesh: float32 [2, 4096, 2048], P(None, 'row', 'col'), may hold values from -6 to 6
- stiffness: float32 [4096, 2048], P('row', 'col'), may hold values from 0.25 to 4
- tissue: int32 [4, 4096, 2048], P(None, 'row', 'col'), may hold values 0 or 1
- flow_blocks: float32 [4, 16384, 2, 256], P(None, ('row', 'col')), may hold values from -8 to 8
- confidence: float32 [4, 16384, 256], P(None, ('row', 'col')), may hold values from 0.25 to 2
- flow_dest: int32 [4, 16384, 1], P(None, ('row', 'col')), may hold values from 0 to 127; in each aligned block of 128 rows (0 to 127, 128 to 255, ..., all dimensions but the last counted through in order) at most 2 rows name the same one
- flow_slot: int32 [4, 16384], P(None, ('row', 'col')), may hold values from 0 to 255
Outputs:
- relaxed: float32 [4, 2, 4096, 2048], P(None, None, 'row', 'col')
Inputs may be any that keep to these rules, and one draw needn't show every extreme that they name: `flow_dest`: among the 128 blocks of one section held by one device, at most 2 name the same tile; in every draw some tile is named exactly 2 times so. Several blocks may land on the same square.
All inputs are finite; a program needn't handle non-finite values. No bound on the sum of `tissue` on one device may be relied on, other than what follows from the above.
Results may differ from a plain program's by a relative error of at most 0.0001.
Values sent between devices are 32-bit elements; how exact they have to be, the bound alone decides.
No kernel may reach another device: no remote copies, remote signals or barrier semaphores. Data moves between devices by JAX's collectives and lax.ppermute only.
A program may use at most 128 MiB of HBM per device.

v0:
```python
from functools import reduce

import jax
import jax.numpy as jnp
from jax import lax
from jax.sharding import PartitionSpec as P

TILE_R = 256
TILE_C = 256
PB = 16
SECTIONS = 4
ITERS = 12
CAP = 2
POS = 256


damping_weight = 0.8
anchor_weight = 0.5
neighbours = (
    (0, 1, 1.0),
    (0, -1, 1.0),
    (1, 0, 1.0),
    (-1, 0, 1.0),
    (1, 1, 0.5),
    (1, -1, 0.5),
    (-1, 1, 0.5),
    (-1, -1, 0.5),
)


def with_halo(cells, sides, width):
    for axis, dim in sides:
        count = lax.axis_size(axis)
        ends = count - 1
        head = lax.slice_in_dim(cells, 0, width, axis=dim)
        tail = lax.slice_in_dim(cells, cells.shape[dim] - width, cells.shape[dim], axis=dim)
        cells = jnp.concatenate(
            [
                lax.ppermute(tail, axis, [(i, (i + 1) % count) for i in range(ends)]),
                cells,
                lax.ppermute(head, axis, [((i + 1) % count, i) for i in range(ends)]),
            ],
            axis=dim,
        )
    return cells


def beside(padded, down, right):
    height = padded.shape[-2] - 2
    width = padded.shape[-1] - 2
    return padded[..., 1 + down : 1 + down + height, 1 + right : 1 + right + width]


def springs(padded_stiff):
    centre = beside(padded_stiff, 0, 0)
    return [
        jnp.sqrt(centre * beside(padded_stiff, down, right)) * share
        for down, right, share in neighbours
    ]


def smoothing(padded):
    terms = [beside(padded, down, right) for down in (-1, 0, 1) for right in (-1, 0, 1)]
    return reduce(jnp.add, terms) / 9.0


def relax(padded, edges, diagonal, target):
    total = target
    for edge, (down, right, share) in zip(edges, neighbours):
        total = total + edge * beside(padded, down, right)
    centre = beside(padded, 0, 0)
    return centre + damping_weight * (total / diagonal - centre)


def pack_blocks(flow, weights, target_tile, place, tiles):
    onehot = (target_tile[:, None] == jnp.arange(tiles, dtype=jnp.int32)[None, :]).astype(jnp.int32)
    before = jnp.cumsum(onehot, axis=0) - onehot
    rank = jnp.sum(before * onehot, axis=1)
    slot_index = target_tile * CAP + rank
    payload = jnp.concatenate([flow * weights[:, None, :], weights[:, None, :]], axis=1)
    buffer = jnp.zeros((tiles * CAP, 3, payload.shape[-1]), jnp.float32).at[slot_index].set(payload)
    places = jnp.zeros((tiles * CAP,), jnp.float32).at[slot_index].set(place.astype(jnp.float32))
    return (buffer, places)


def shards(anchor_mesh, stiffness, tissue, flow_blocks, confidence, flow_dest, flow_slot):
    rows = lax.axis_size("row")
    columns = lax.axis_size("col")
    tiles = rows * columns
    depth = 1
    padded_stiff = with_halo(stiffness, (("row", 0), ("col", 1)), depth)
    edges = springs(padded_stiff)
    total_edges = reduce(jnp.add, edges)
    previous = anchor_mesh
    results = []
    for section in range(SECTIONS):
        buffer, places = pack_blocks(
            flow_blocks[section],
            confidence[section],
            flow_dest[section, :, 0],
            flow_slot[section],
            tiles,
        )
        arrived, spots = (
            lax.all_to_all(
                buffer.reshape(tiles, CAP, 3, buffer.shape[-1]),
                ("row", "col"),
                split_axis=0,
                concat_axis=0,
                tiled=True,
            ),
            lax.all_to_all(
                places.reshape(tiles, CAP), ("row", "col"), split_axis=0, concat_axis=0, tiled=True
            ),
        )
        summed = jax.ops.segment_sum(
            arrived.reshape(-1, 3, arrived.shape[-1]),
            spots.reshape(-1).astype(jnp.int32),
            num_segments=POS,
        )
        grid = (
            summed.reshape(TILE_R // PB, TILE_C // PB, 3, PB, PB)
            .transpose(2, 0, 3, 1, 4)
            .reshape(3, TILE_R, TILE_C)
        )
        mask = tissue[section].astype(jnp.float32)
        flow_field = jnp.concatenate([grid[:2] * mask, (grid[2] * mask)[None]], axis=0)
        pulled = flow_field[:2]
        weight = flow_field[2]
        padded_previous = with_halo(previous, (("row", 1), ("col", 2)), depth)
        smooth = smoothing(padded_previous)
        diagonal = total_edges + weight + anchor_weight
        target = pulled + anchor_weight * smooth

        def group_step(index, field):
            padded = with_halo(field, (("row", 1), ("col", 2)), depth)
            padded = relax(padded, [edge for edge in edges], diagonal, target)
            return padded

        field = lax.fori_loop(0, ITERS // depth, group_step, previous)
        results.append(field)
        previous = field
    return jnp.stack(results)


def solution(mesh):
    placed = (
        P(None, "row", "col"),
        P("row", "col"),
        P(None, "row", "col"),
        P(None, ("row", "col"), None, None),
        P(None, ("row", "col"), None),
        P(None, ("row", "col"), None),
        P(None, ("row", "col")),
    )
    return jax.shard_map(
        shards, mesh=mesh, in_specs=placed, out_specs=P(None, None, "row", "col"), check_vma=False
    )
```

profile of v0, /device:TPU:30, one launch (start us, length us, event | category | flops | bytes accessed | tf_op | source)
XLA Modules:
  0.0 1551.7 jit_solution(8173872104272059782)
XLA Ops:
  5.9 10.2 all-to-all-start.6
  17.9 4.8 all-to-all-done.6
  22.7 7.5 all-to-all-start
  32.7 4.1 all-to-all-done
  36.9 7.5 all-to-all-start.2
  50.9 7.5 all-to-all-start.4
  59.0 4.4 scatter_fusion.6
  65.0 9.4 all-to-all-start.7
  74.6 4.4 scatter_fusion.4
  80.3 7.4 all-to-all-done.7
  87.7 7.7 all-to-all-start.5
  100.3 4.3 collective-permute-start.17
  107.1 6.2 collective-permute-start.20
  117.1 8.8 scatter_fusion
  127.4 4.4 scatter_fusion.2
  133.2 6.8 all-to-all-start.1
  142.5 10.8 all-to-all-done.1
  153.3 8.7 all-to-all-start.3
  178.1 9.6 scatter_fusion.1
  187.8 4.0 reshape.286
  194.9 4.8 slice.622
  200.1 9.2 scatter_fusion.5
  211.0 9.2 scatter_fusion.7
  222.8 9.2 scatter_fusion.3
  232.1 3.9 reshape.289
  240.0 5.9 copy.62
  245.9 4.4 slice.505
  255.4 4.1 reshape.295
  263.4 5.0 reshape.292
  278.2 285.1 %while.40 = (s32[]{:T(128)}, f32[2,256,256]{2,1,0:T(8,128)S(1)}, f32[256,256]{1,0:T(8,128)S(1)}, f32[2,256,256]{2,1,0:T(8,128)}, f32[256,256]{1,0:T(8,128)S(1)},...) while((s32[]{:T(128)}, f32[2,256,256]{2,1,0:T(8,128)S(1)}, ...), condition=%wide.region_6.7_spmd, body=%wide.region_5.6_spmd.sunk | while | flops 3943450 | bytes 10830365 | solution.py:140
  278.2 5.6 collective-permute-start
  285.8 5.6 collective-permute-done.1
  331.2 3.9 collective-permute-start.1
  354.6 3.9 collective-permute-start.1
  378.0 3.9 collective-permute-start.1
  401.4 3.9 collective-permute-start.1
  424.8 3.9 collective-permute-start.1
  448.2 3.9 collective-permute-start.1
  471.6 3.9 collective-permute-start.1
  495.0 3.9 collective-permute-start.1
  518.5 3.9 collective-permute-start.1
  541.9 3.9 collective-permute-start.1
  565.2 6.0 collective-permute-start.25
  592.6 297.5 %while.41 = (s32[]{:T(128)}, f32[2,256,256]{2,1,0:T(8,128)}, f32[256,256]{1,0:T(8,128)S(1)}, f32[2,256,256]{2,1,0:T(8,128)}, f32[256,256]{1,0:T(8,128)S(1)}, /*i...) while((s32[]{:T(128)}, f32[2,256,256]{2,1,0:T(8,128)}, ...), condition=%wide.region_13.14_spmd, body=%wide.region_12.13_spmd.sunk | while | flops 3943450 | bytes 13976149 | solution.py:140
  593.7 6.3 collective-permute-start.4
  601.9 5.6 collective-permute-done.5
  673.2 3.9 collective-permute-start.5
  795.4 3.9 collective-permute-start.5
  844.2 3.9 collective-permute-start.5
  892.8 6.0 collective-permute-start.29
  914.0 4.3 slice.553
  921.8 297.1 %while.42 = (s32[]{:T(128)}, f32[2,256,256]{2,1,0:T(8,128)}, f32[256,256]{1,0:T(8,128)S(1)}, f32[2,256,256]{2,1,0:T(8,128)}, f32[256,256]{1,0:T(8,128)S(1)}, /*i...) while((s32[]{:T(128)}, f32[2,256,256]{2,1,0:T(8,128)}, ...), condition=%wide.region_20.21_spmd, body=%wide.region_19.20_spmd.sunk | while | flops 3943450 | bytes 13976149 | solution.py:140
  922.9 6.3 collective-permute-start.8
  931.1 5.6 collective-permute-done.9
  1026.7 3.9 collective-permute-start.9
  1099.9 3.9 collective-permute-start.9
  1173.1 3.9 collective-permute-start.9
  1221.6 6.0 collective-permute-start.33
  1243.0 4.3 slice.573
  1250.9 297.6 %while.43 = (s32[]{:T(128)}, f32[2,256,256]{2,1,0:T(8,128)}, f32[256,256]{1,0:T(8,128)S(1)}, f32[2,256,256]{2,1,0:T(8,128)}, f32[256,256]{1,0:T(8,128)S(1)}, /*i...) while((s32[]{:T(128)}, f32[2,256,256]{2,1,0:T(8,128)}, ...), condition=%wide.region_27.28_spmd, body=%wide.region_26.27_spmd.sunk | while | flops 3943450 | bytes 12927545 | solution.py:140
  1251.9 6.3 collective-permute-start.12
  1260.2 5.6 collective-permute-done.13
  1356.0 3.9 collective-permute-start.13
  1380.4 3.9 collective-permute-start.13
  (989 shorter events, 1207.9 us)
Async XLA Ops:
  5.9 16.8 %all-to-all-start.6 = ((f32[128,1,2]{2,1,0:T(1,128)}), f32[128,1,2]{2,1,0:T(1,128)S(1)}, u32[]{:S(2)}, u32[]{:S(2)}) async-start(f32[128,1,2]{2,1,0:T(1,128)} %bitcast.47), calls=%async_computation.6 | async-start | bytes 131072 | tf_op jit(solution)/shard_map/all_to_all | solution.py:112
  22.7 14.1 all-to-all-start
  36.9 14.0 all-to-all-start.2
  50.9 14.1 all-to-all-start.4
  65.0 22.7 %all-to-all-start.7 = ((f32[128,2,3,256]{3,1,2,0:T(2,128)}), f32[128,2,3,256]{3,1,2,0:T(2,128)S(1)}, u32[]{:S(2)}, u32[]{:S(2)}) async-start(f32[128,2,3,256]{3,1,2,0:T(2,128)} %copy.82), calls=%async_computation.7 | async-start | bytes 1572864 | tf_op jit(solution)/shard_map/all_to_all | solution.py:105
  87.7 45.5 %all-to-all-start.5 = ((f32[128,2,3,256]{3,1,2,0:T(2,128)}), f32[128,2,3,256]{3,1,2,0:T(2,128)S(1)}, u32[]{:S(2)}, u32[]{:S(2)}) async-start(f32[128,2,3,256]{3,1,2,0:T(2,128)} %copy.74), calls=%async_computation.5 | async-start | bytes 1572864 | tf_op jit(solution)/shard_map/all_to_all | solution.py:105
  96.7 45.7 %collective-permute-start.16 = (f32[1,256]{1,0:T(1,128)}, f32[1,256]{1,0:T(1,128)S(1)}, u32[]{:S(2)}, u32[]{:S(2)}) collective-permute-start(f32[1,256]{1,0:T(1,128)} %get-tuple-element.434), channel_id=1, source_target_pairs={{0,8},{8,16},{16,24},{24,32},{32,40},{40,48},{48,56},{56,64},{64,7... | collective-permute-start | bytes 3080 | tf_op jit(solution)/shard_map/ppermute | solution.py:39
  100.3 42.1 %collective-permute-start.17 = (f32[1,256]{1,0:T(1,128)}, f32[1,256]{1,0:T(1,128)S(1)}, u32[]{:S(2)}, u32[]{:S(2)}) collective-permute-start(f32[1,256]{1,0:T(1,128)} %get-tuple-element.435), channel_id=1, source_target_pairs={{8,0},{16,8},{24,16},{32,24},{40,32},{48,40},{56,48},{64,56},{72,6... | collective-permute-start | bytes 3080 | tf_op jit(solution)/shard_map/ppermute | solution.py:41
  105.2 61.3 %collective-permute-start.19 = (f32[2,1,256]{2,1,0:T(1,128)}, f32[2,1,256]{2,1,0:T(1,128)S(1)}, u32[]{:S(2)}, u32[]{:S(2)}) collective-permute-start(f32[2,1,256]{2,1,0:T(1,128)} %get-tuple-element.428), channel_id=1, source_target_pairs={{0,8},{8,16},{16,24},{24,32},{32,40},{40,48},{48,56},{56,64},{64,7... | collective-permute-start | bytes 6152 | tf_op jit(solution)/shard_map/ppermute | solution.py:39
  107.1 59.4 %collective-permute-start.20 = (f32[2,1,256]{2,1,0:T(1,128)}, f32[2,1,256]{2,1,0:T(1,128)S(1)}, u32[]{:S(2)}, u32[]{:S(2)}) collective-permute-start(f32[2,1,256]{2,1,0:T(1,128)} %get-tuple-element.429), channel_id=1, source_target_pairs={{8,0},{16,8},{24,16},{32,24},{40,32},{48,40},{56,48},{64,56},{72,6... | collective-permute-start | bytes 6152 | tf_op jit(solution)/shard_map/ppermute | solution.py:41
  133.2 20.1 %all-to-all-start.1 = ((f32[128,2,3,256]{3,1,2,0:T(2,128)}), f32[128,2,3,256]{3,1,2,0:T(2,128)S(1)}, u32[]{:S(2)}, u32[]{:S(2)}) async-start(f32[128,2,3,256]{3,1,2,0:T(2,128)} %copy.58), calls=%async_computation.1 | async-start | bytes 1572864 | tf_op jit(solution)/shard_map/all_to_all | solution.py:105
  153.3 68.0 %all-to-all-start.3 = ((f32[128,2,3,256]{3,1,2,0:T(2,128)}), f32[128,2,3,256]{3,1,2,0:T(2,128)}, u32[]{:S(2)}, u32[]{:S(2)}) async-start(f32[128,2,3,256]{3,1,2,0:T(2,128)} %copy.66), calls=%async_computation.3 | async-start | bytes 1572864 | tf_op jit(solution)/shard_map/all_to_all | solution.py:105
  162.1 10.2 collective-permute-start.18
  164.6 8.0 collective-permute-start.23
  166.7 8.8 collective-permute-start.21
  458.6 7.9 collective-permute-start.3
  563.3 8.0 collective-permute-start.24
  573.5 16.3 %collective-permute-start.26 = (f32[2,258,1]{2,1,0:T(8,128)}, f32[2,258,1]{2,1,0:T(8,128)}, u32[]{:S(2)}, u32[]{:S(2)}) collective-permute-start(f32[2,258,1]{2,1,0:T(8,128)} %get-tuple-element.402), channel_id=1, source_target_pairs={{0,1},{1,2},{2,3},{3,4},{4,5},{5,6},{6,7},{8,9},{9,10},{10,11},{11... | collective-permute-start | bytes 6200 | tf_op jit(solution)/shard_map/ppermute | solution.py:39
  575.4 14.4 collective-permute-start.27
  593.7 8.2 collective-permute-start.4
  610.4 8.1 collective-permute-start.7
  634.8 8.1 collective-permute-start.7
  659.2 8.1 collective-permute-start.7
  683.7 8.1 collective-permute-start.7
  708.1 8.1 collective-permute-start.7
  732.5 8.1 collective-permute-start.7
  756.9 8.1 collective-permute-start.7
  781.4 8.1 collective-permute-start.7
  805.8 8.1 collective-permute-start.7
  830.2 8.1 collective-permute-start.7
  854.7 8.1 collective-permute-start.7
  879.1 8.1 collective-permute-start.7
  890.9 8.0 collective-permute-start.28
  902.1 17.0 %collective-permute-start.30 = (f32[2,258,1]{2,1,0:T(8,128)}, f32[2,258,1]{2,1,0:T(8,128)}, u32[]{:S(2)}, u32[]{:S(2)}) collective-permute-start(f32[2,258,1]{2,1,0:T(8,128)} %get-tuple-element.400), channel_id=1, source_target_pairs={{0,1},{1,2},{2,3},{3,4},{4,5},{5,6},{6,7},{8,9},{9,10},{10,11},{11... | collective-permute-start | bytes 6200 | tf_op jit(solution)/shard_map/ppermute | solution.py:39
  904.0 15.1 collective-permute-start.31
  922.9 8.2 collective-permute-start.8
  939.6 8.1 collective-permute-start.11
  964.0 8.1 collective-permute-start.11
  988.4 8.1 collective-permute-start.11
  1012.8 8.1 collective-permute-start.11
  1037.2 8.1 collective-permute-start.11
  1061.6 8.1 collective-permute-start.11
  1086.0 8.1 collective-permute-start.11
  1110.3 8.1 collective-permute-start.11
  1134.7 8.1 collective-permute-start.11
  1159.1 8.1 collective-permute-start.11
  1183.5 8.1 collective-permute-start.11
  1207.9 8.1 collective-permute-start.11
  1219.6 8.0 collective-permute-start.32
  1230.9 17.2 %collective-permute-start.34 = (f32[2,258,1]{2,1,0:T(8,128)}, f32[2,258,1]{2,1,0:T(8,128)}, u32[]{:S(2)}, u32[]{:S(2)}) collective-permute-start(f32[2,258,1]{2,1,0:T(8,128)} %get-tuple-element.398), channel_id=1, source_target_pairs={{0,1},{1,2},{2,3},{3,4},{4,5},{5,6},{6,7},{8,9},{9,10},{10,11},{11... | collective-permute-start | bytes 6200 | tf_op jit(solution)/shard_map/ppermute | solution.py:39
  1232.8 15.3 collective-permute-start.35
  1251.9 8.2 collective-permute-start.12
  1268.7 8.1 collective-permute-start.15
  1293.1 8.1 collective-permute-start.15
  1317.5 8.1 collective-permute-start.15
  1342.0 8.1 collective-permute-start.15
  1366.4 8.1 collective-permute-start.15
  1390.8 8.1 collective-permute-start.15
  1415.3 8.1 collective-permute-start.15
  1439.7 8.1 collective-permute-start.15
  1464.2 8.1 collective-permute-start.15
  1488.6 8.1 collective-permute-start.15
  1513.0 8.1 collective-permute-start.15
  1537.5 8.1 collective-permute-start.15
  (254 other events, 1768.9 us)
where the time goes:
time: 1570 us; the launch traced here: 1550 us
  starting transfers between devices  662 us (42%)
  waiting for transfers between devices  457 us (29%)
  local copies, waits for them, and re-layouts  217 us (14%)
  other arithmetic  210 us (13%)
    ppermute x106, waiting for transfers between devices, with_halo(): lax.ppermute(tail, axis, [(i, (i + 1) % count) for i in range(ends)])  366 us
    ppermute x106, starting transfers between devices, with_halo(): lax.ppermute(tail, axis, [(i, (i + 1) % count) for i in range(ends)])  350 us
    ppermute x106, starting transfers between devices, with_halo(): lax.ppermute(head, axis, [((i + 1) % count, i) for i in range(ends)])  247 us
    add x48, other arithmetic, relax(): return centre + damping_weight * (total / diagonal - centre)  77.6 us
    concatenate x106, other arithmetic, with_halo(): jnp.concatenate([lax.ppermute(tail, axis, [(i, (i + 1) % count) for i in...  75.7 us
    ppermute x106, waiting for transfers between devices, with_halo(): lax.ppermute(head, axis, [((i + 1) % count, i) for i in range(ends)])  59.9 us
    slice x12, local copies, waits for them, and re-layouts, shards(): grid[:2] * mask  46.1 us
    slice x49, local copies, waits for them, and re-layouts, with_halo(): head = lax.slice_in_dim(cells, 0, width, axis=dim)  41.2 us
  transfers between devices with their start and end apart: 220, of which 156 were waited for; matrix products, arithmetic and copies ran while one was open for 8% of the time, Pallas kernels for 0%

commit v1 on v0

v1 whole, which is shorter than its diff:
```python
import jax
import jax.numpy as jnp
from jax import lax
from jax.experimental import pallas as pl
from jax.experimental.pallas import tpu as pltpu
from jax.sharding import PartitionSpec as P

SECTIONS = 4
ITERS = 12
TILES = 128
GROUP = (0, 1, 2, 3)
HALO = 48
WIDTHS = (48, 40, 24, 16)
LANES = (48, 36, 24, 12)
STEPS = 45
ROWS = 8 * STEPS
PITCH = 17
LINES = 49
ALL_WIDTHS = tuple(width for width in WIDTHS for _ in range(3)) + (HALO,) * 3
ALL_LANES = tuple(width for width in LANES for _ in range(3)) + (HALO,) * 3
DEPTH = 4

damping_weight = 0.8
anchor_weight = 0.5

f32 = jnp.float32
bf16 = jnp.bfloat16
VMEM_LIMIT = 24 * 1024 * 1024


def call(body, name, cost, out_shape, count, limit=VMEM_LIMIT, **more):
    if "in_specs" not in more:
        more["in_specs"] = whole(count)
    return pl.pallas_call(
        body,
        out_shape=out_shape,
        compiler_params=pltpu.CompilerParams(vmem_limit_bytes=limit),
        cost_estimate=pl.CostEstimate(flops=0, bytes_accessed=cost, transcendentals=0),
        name=name,
        **more,
    )


def whole(count):
    return [pl.BlockSpec(memory_space=pltpu.VMEM)] * count


def iota(shape, dim):
    return lax.broadcasted_iota(jnp.int32, shape, dim)


def ones_where(mask):
    return jnp.where(mask, 1.0, 0.0).astype(bf16)


def dot(a, b):
    return jnp.dot(a, b, preferred_element_type=f32)


def turned_dot(a, b):
    return lax.dot_general(a, b, (((1,), (1,)), ((), ())), preferred_element_type=f32)


def two_terms(a):
    high = a.astype(bf16)
    return jnp.concatenate([high, (a - high.astype(f32)).astype(bf16)], axis=0)


def earlier():
    return ones_where(iota((TILES, 128), 0) < iota((TILES, 128), 1))


def pack_kernel(group, flow_hbm, conf_hbm, dest_ref, slot_ref, out_ref, flow_ref, conf_ref, sems):
    copies = []
    for k, s in enumerate(group):
        copies.append(
            (
                pltpu.make_async_copy(conf_hbm.at[s], conf_ref.at[k], sems.at[2 * k]),
                pltpu.make_async_copy(flow_hbm.at[s], flow_ref.at[k], sems.at[2 * k + 1]),
            )
        )
        for copy in copies[-1]:
            copy.start()
    row_of = iota((TILES, 128), 0)
    before = earlier()
    places = jnp.zeros((TILES, 128), f32)
    for k, s in enumerate(group):
        named = row_of == dest_ref[s : s + 1, :]
        rank = dot(ones_where(named), before)
        ranked = [ones_where(named & (rank < 0.5)), ones_where(named & (rank > 0.5))]
        chosen = jnp.concatenate(ranked, axis=0)
        chosen = jnp.concatenate([chosen, chosen], axis=1)
        slot = slot_ref[s : s + 1, :].astype(f32)
        for r in range(2):
            places = places + turned_dot(ranked[r], jnp.where(row_of == 2 * k + r, slot, 0.0).astype(bf16))
        for copy in copies[k]:
            copy.wait()
        halves = [conf_ref[k, :, 128 * h : 128 * h + 128] for h in range(2)]
        for pair in range(3):
            if pair < 2:
                parts = [
                    halves[pair] * flow_ref[k, pl.ds(2 * pair + c, TILES, stride=4), :] for c in range(2)
                ]
            else:
                parts = halves
            sent = dot(chosen, two_terms(jnp.concatenate(parts, axis=1)))
            for r in range(2):
                for c in range(2):
                    out_ref[pl.ds(12 * k + 6 * r + 2 * pair + c, TILES, stride=LINES), :] = sent[
                        TILES * r : TILES * r + TILES, 128 * c : 128 * c + 128
                    ]
    out_ref[pl.ds(LINES - 1, TILES, stride=LINES), :] = places


def pack(group, flow, conf, dest, slot, limit=VMEM_LIMIT):
    count = len(group)
    return call(
        lambda *refs: pack_kernel(group, *refs),
        "pack",
        8 << 20,
        jax.ShapeDtypeStruct((TILES * LINES, 128), f32),
        4,
        limit=limit,
        in_specs=[pl.BlockSpec(memory_space=pltpu.HBM)] * 2 + whole(2),
        scratch_shapes=[
            pltpu.VMEM((count, 4 * TILES, 128), f32),
            pltpu.VMEM((count, TILES, 256), f32),
            pltpu.SemaphoreType.DMA((2 * count,)),
        ],
    )(flow, conf, dest, slot)


def exchanged_groups(v, lane):
    v = list(v)
    for bit in (4, 2, 1):
        right = (lane & (16 * bit)) != 0
        for a in range(8):
            if a & bit == 0:
                b = a | bit
                v[a], v[b] = (
                    jnp.where(right, pltpu.roll(v[b], 16 * bit, 1), v[a]),
                    jnp.where(right, v[b], pltpu.roll(v[a], 128 - 16 * bit, 1)),
                )
    return v


def land_kernel(group, arrived_ref, tissue_ref, *refs):
    *extras, out_ref, top_ref, bottom_ref, cells_ref = refs
    row = iota((256, TILES), 0)
    squares = ((row >> 7) * 128 + (row & 7) * 16 + ((row >> 3) & 15)).astype(f32)
    lane = iota((8, 128), 1)
    places = arrived_ref[pl.ds(LINES - 1, TILES, stride=LINES), :].astype(bf16)
    places = turned_dot(ones_where(iota((8, 128), 0) == iota((8, 128), 1)), places)
    offset = 0
    for k, s in enumerate(group):
        here = [ones_where(squares == places[2 * k + r : 2 * k + r + 1, :]) for r in range(2)]
        here = jnp.concatenate(here + here, axis=1)
        for pair in range(3):
            part = jnp.concatenate(
                [
                    jnp.concatenate(
                        [
                            arrived_ref[pl.ds(12 * k + 6 * r + 2 * pair + c, TILES, stride=LINES), :]
                            for c in range(2)
                        ],
                        axis=1,
                    )
                    for r in range(2)
                ],
                axis=0,
            )
            summed = dot(here, two_terms(part))
            for c in range(2):
                comp, half = (c, pair) if pair < 2 else (2, c)
                cells = summed[:, 128 * c : 128 * c + 128].reshape(2, 2, 8, 8, 128)
                for high in range(2):
                    for side in range(2):
                        turned = exchanged_groups([cells[high, side, i] for i in range(8)], lane)
                        for r in range(8):
                            rows = pl.ds(8 * PITCH * high + 8 * half + r, 8, stride=PITCH)
                            cells_ref[k, comp, side, rows, :] = turned[r]
        for side in range(2):
            for r in range(16):
                rows = slice(16 * r, 16 * r + 16)
                mask = tissue_ref[s, rows, 128 * side : 128 * side + 128].astype(f32)
                for comp in range(3):
                    value = cells_ref[k, comp, side, PITCH * r : PITCH * r + 16, :] * mask
                    out_ref[3 * k + comp, side, rows, :] = value
        width = WIDTHS[k]
        for comp in range(3):
            for side in range(2):
                cols = slice(128 * side, 128 * side + 128)
                top_ref[offset : offset + width, cols] = out_ref[3 * k + comp, side, :width, :]
                bottom_ref[offset : offset + width, cols] = out_ref[3 * k + comp, side, 256 - width :, :]
            offset += width
    for ref in extras:
        for i in range(ref.shape[0]):
            top_ref[offset : offset + HALO] = ref[i, :HALO]
            bottom_ref[offset : offset + HALO] = ref[i, 256 - HALO :]
            offset += HALO


def land(group, arrived, tissue, extras):
    count = len(group)
    strip = sum(ALL_WIDTHS)
    operands = [arrived, tissue, *extras]
    return call(
        lambda *refs: land_kernel(group, *refs),
        "land",
        16 << 20,
        [
            jax.ShapeDtypeStruct((count * 3, 2, 256, 128), f32),
            jax.ShapeDtypeStruct((strip, 256), f32),
            jax.ShapeDtypeStruct((strip, 256), f32),
        ],
        len(operands),
        scratch_shapes=[pltpu.VMEM((count, 3, 2, 16 * PITCH, 128), f32)],
    )(*operands)


def arranged(lanes):
    used, where = [], {}
    for width, i in sorted(((width, i) for i, width in enumerate(lanes)), key=lambda pair: -pair[0]):
        for half in range(2):
            block = next((n for n, taken in enumerate(used) if taken + width <= 128), len(used))
            if block == len(used):
                used.append(0)
            where[i, half] = (block, used[block])
            used[block] += width
    return where, len(used)


def plane_of(ref, i, rows, side):
    if len(ref.shape) == 4:
        return ref[i, side, rows, :]
    return ref[i, rows, 128 * side : 128 * side + 128]


def merge_strips(out_refs, height, strip_of):
    lane = iota((height, 128), 1)
    where, blocks = arranged(ALL_LANES)
    for side, out_ref in enumerate(out_refs):
        for block in range(blocks):
            merged = jnp.zeros((height, 128), f32)
            for (i, half), (at, offset) in where.items():
                if at != block:
                    continue
                strip = strip_of(i, half, side)
                turn = (offset + ALL_LANES[i] * side) % 128
                if turn:
                    strip = pltpu.roll(strip, turn, 1)
                merged = jnp.where((lane >= offset) & (lane < offset + ALL_LANES[i]), strip, merged)
            out_ref[block] = merged


def column_kernel(*refs):
    *own_refs, first_ref, last_ref = refs
    own = [(ref, i) for ref in own_refs for i in range(ref.shape[0])]

    def strip_of(i, half, side):
        ref, n = own[i]
        return plane_of(ref, n, slice(128 * half, 128 * half + 128), side)

    merge_strips((first_ref, last_ref), 128, strip_of)


def corner_kernel(above_ref, below_ref, first_ref, last_ref):
    starts = [sum(ALL_WIDTHS[:i]) for i in range(len(ALL_WIDTHS))]

    def strip_of(i, half, side):
        ref = below_ref if half else above_ref
        width = ALL_WIDTHS[i]
        strip = ref[starts[i] : starts[i] + width, 128 * side : 128 * side + 128]
        if width < HALO:
            strip = jnp.concatenate([strip, jnp.zeros((HALO - width, 128), f32)], axis=0)
        return strip

    merge_strips((first_ref, last_ref), HALO, strip_of)


def strips_of(kernel, name, height, operands):
    blocks = arranged(ALL_LANES)[1]
    return call(
        kernel,
        name,
        4 << 20,
        [jax.ShapeDtypeStruct((blocks, height, 128), f32)] * 2,
        len(operands),
        out_specs=whole(2),
    )(*operands)


def shifted(cells, axis, step):
    count = lax.axis_size(axis)
    pairs = [(i, i + step) for i in range(count) if 0 <= i + step < count]
    return lax.ppermute(cells, axis, pairs)


def ring(own, top, bottom):
    below = shifted(top, "row", -1)
    above = shifted(bottom, "row", 1)
    first, last = strips_of(column_kernel, "columns", 128, own)
    right = shifted(first, "col", -1)
    left = shifted(last, "col", 1)
    first, last = strips_of(corner_kernel, "corners", HALO, [above, below])
    right_corners = shifted(first, "col", -1)
    left_corners = shifted(last, "col", 1)
    return above, below, right, left, right_corners, left_corners


def fill(ext_ref, index, own, number, strips):
    above_ref, below_ref, *side_refs = strips
    own_ref, i = own
    width, start = ALL_WIDTHS[number], sum(ALL_WIDTHS[:number])
    where = arranged(ALL_LANES)[0]
    for plane in range(2):
        cols = slice(128 * plane, 128 * plane + 128)
        ext_ref[index, plane, HALO - width : HALO, :] = above_ref[start : start + width, cols]
        ext_ref[index, plane, HALO : HALO + 256, :] = plane_of(own_ref, i, slice(0, 256), plane)
        ext_ref[index, plane, HALO + 256 : HALO + 256 + width, :] = below_ref[start : start + width, cols]
    for half in range(2):
        at, offset = where[number, half]
        for refs, first, rows in (
            (side_refs[:2], HALO + 128 * half, 128),
            (side_refs[2:], HALO + 256 if half else HALO - width, width),
        ):
            right, left = refs[0][at, :rows, :], refs[1][at, :rows, :]
            if offset:
                right = pltpu.roll(right, 128 - offset, 1)
            if (offset + ALL_LANES[number]) % 128:
                left = pltpu.roll(left, 128 - offset - ALL_LANES[number], 1)
            near = iota((rows, 128), 1) < 64
            ext_ref[index, 2, first : first + rows, :] = jnp.where(near, right, left)


def spread(t):
    return pl.ds(t, 8, stride=STEPS)


def block(t):
    return slice(8 * t, 8 * t + 8)


def three(ref, index, t):
    if t < 0:
        return [pltpu.roll(v, 1, 0) for v in three(ref, index, STEPS - 1)]
    if t == STEPS:
        return [pltpu.roll(v, 7, 0) for v in three(ref, index, 0)]
    return [ref[index + (j, block(t))] for j in range(3)]


def walk(sources, body, late=1):
    here = [three(ref, index, 0) for ref, index in sources]
    above = [
        [p + q for p, q in zip(three(ref, index, -1), planes)]
        for (ref, index), planes in zip(sources, here)
    ]
    waiting = []
    for t in range(STEPS):
        ahead = [three(ref, index, t + 1) for ref, index in sources]
        below = [[p + q for p, q in zip(a, b)] for a, b in zip(here, ahead)]
        waiting.append(body(t, list(zip(here, above, below))))
        here, above = ahead, below
        if len(waiting) > late:
            for ref, at, value in waiting.pop(0):
                ref[at] = value
    for stores in waiting:
        for ref, at, value in stores:
            ref[at] = value


def relax_kernel(group, *refs):
    field_own, stiff_own, flow_own, *rest = refs
    strips, rest = rest[:6], rest[6:]
    out_ref, x_ref, g_ref, gi_ref, d_ref, f_ref, u0_ref, u1_ref, a_ref, c_ref, b_ref, stage_ref, sems = rest
    lane = iota((8, 128), 1)
    first_lane = lane == 0
    last_lane = lane == 127

    def from_left(planes):
        turned = [pltpu.roll(v, 1, 1) for v in planes]
        return [jnp.where(first_lane, turned[(j + 2) % 3], turned[j]) for j in range(3)]

    def from_right(planes):
        turned = [pltpu.roll(v, 127, 1) for v in planes]
        return [jnp.where(last_lane, turned[(j + 1) % 3], turned[j]) for j in range(3)]

    def weighted(above, below):
        v = [p + q for p, q in zip(above, below)]
        return [(p + q) + (w + w) for p, q, w in zip(from_left(v), from_right(v), v)]

    for c in range(2):
        fill(x_ref, c, (field_own, c), 3 * len(group) + c, strips)
    fill(x_ref, 2, (stiff_own, 0), 3 * len(group) + 2, strips)
    for t in range(STEPS):
        for j in range(3):
            stiff = x_ref[2, j, spread(t), :]
            root = jnp.sqrt(stiff)
            inside = stiff > 0
            g_ref[j, block(t), :] = root
            gi_ref[j, block(t), :] = jnp.where(inside, 1.0 / jnp.where(inside, root, 1.0), 0.0)
            for c in range(2):
                value = x_ref[c, j, spread(t), :]
                f_ref[c, j, block(t), :] = value
                u0_ref[c, j, block(t), :] = root * value

    def stiffness_sums(t, sources):
        ((here, above, below),) = sources
        z = weighted(above, below)
        return [
            (d_ref, (j, block(t)), here[j] * (0.5 * z[j] - 2.0 * here[j]) + anchor_weight)
            for j in range(3)
        ]

    walk([(g_ref, ())], stiffness_sums)

    copies = []
    for k, s in enumerate(group):
        for i in range(3):
            fill(x_ref, i, (flow_own, 3 * k + i), 3 * k + i, strips)

        def coefficients(t, sources):
            stores = []
            wg = []
            for j in range(3):
                root = g_ref[j, block(t), :]
                w = damping_weight / (d_ref[j, block(t), :] + x_ref[2, j, spread(t), :])
                wg.append(w * root)
                a = (0.5 * wg[j]) * root
                stores.append((a_ref, (j, block(t)), a))
                stores.append((c_ref, (j, block(t)), (1.0 - damping_weight) - 4.0 * a))
            for c, (here, above, below) in enumerate(sources):
                v = [(p + q) - h for p, q, h in zip(above, below, here)]
                sides = [p + q for p, q in zip(from_left(v), from_right(v))]
                for j in range(3):
                    target = x_ref[c, j, spread(t), :] + (anchor_weight / 9.0) * (sides[j] + v[j])
                    stores.append((b_ref, (c, j, block(t)), wg[j] * target))
            return stores

        walk([(f_ref, (c,)) for c in range(2)], coefficients)

        def sweep(src_ref, dst_ref):
            here = [three(src_ref, (c,), 0) for c in range(2)]
            above = [
                [p + q for p, q in zip(three(src_ref, (c,), -1), here[c])] for c in range(2)
            ]
            begun = []
            for t in range(STEPS + DEPTH):
                if t < STEPS:
                    ahead = [three(src_ref, (c,), t + 1) for c in range(2)]
                    below = [[p + q for p, q in zip(here[c], ahead[c])] for c in range(2)]
                    entry = []
                    a = [a_ref[j, block(t), :] for j in range(3)]
                    keep = [c_ref[j, block(t), :] for j in range(3)]
                    twice = [w + w for w in a]
                    for c in range(2):
                        v = [p + q for p, q in zip(above[c], below[c])]
                        right = [pltpu.roll(w, 1, 1) for w in v]
                        left = [pltpu.roll(w, 127, 1) for w in v]
                        known = [
                            (keep[j] * here[c][j] + b_ref[c, j, block(t), :]) + twice[j] * v[j]
                            for j in range(3)
                        ]
                        entry.append((known, right, left))
                    begun.append(entry)
                    here, above = ahead, below
                if t >= DEPTH:
                    at = t - DEPTH
                    a = [a_ref[j, block(at), :] for j in range(3)]
                    for c, (known, right, left) in enumerate(begun.pop(0)):
                        for j in range(3):
                            sides = jnp.where(first_lane, right[(j + 2) % 3], right[j]) + jnp.where(
                                last_lane, left[(j + 1) % 3], left[j]
                            )
                            dst_ref[c, j, block(at), :] = known[j] + a[j] * sides

        def two(i, carry):
            sweep(u0_ref, u1_ref)
            sweep(u1_ref, u0_ref)
            return carry

        lax.fori_loop(0, ITERS // 2, two, 0)

        for t in range(STEPS):
            for j in range(3):
                inverse = gi_ref[j, block(t), :]
                for c in range(2):
                    value = inverse * u0_ref[c, j, block(t), :]
                    f_ref[c, j, block(t), :] = value
                    x_ref[c, j, spread(t), :] = value
        for c in range(2):
            for j in range(2):
                cols = slice(128 * j, 128 * j + 128)
                value = x_ref[c, j, HALO : HALO + 256, :]
                stage_ref[k, c, :, cols] = value
        copy = pltpu.make_async_copy(stage_ref.at[k], out_ref.at[s], sems.at[k])
        copy.start()
        copies.append(copy)
    for copy in copies:
        copy.wait()


def relax(group, field, stiffness, flow, strips):
    ext = (3, ROWS, 128)
    operands = [field, stiffness, flow, *strips]
    return call(
        lambda *refs: relax_kernel(group, *refs),
        "relax",
        96 << 20,
        jax.ShapeDtypeStruct((SECTIONS, 2, 256, 256), f32),
        len(operands),
        out_specs=pl.BlockSpec(memory_space=pl.ANY),
        scratch_shapes=[
            pltpu.VMEM((3,) + ext, f32),
            pltpu.VMEM(ext, f32),
            pltpu.VMEM(ext, f32),
            pltpu.VMEM(ext, f32),
            pltpu.VMEM((2,) + ext, f32),
            pltpu.VMEM((2,) + ext, f32),
            pltpu.VMEM((2,) + ext, f32),
            pltpu.VMEM(ext, f32),
            pltpu.VMEM(ext, f32),
            pltpu.VMEM((2,) + ext, f32),
            pltpu.VMEM((len(group), 2, 256, 256), f32),
            pltpu.SemaphoreType.DMA((len(group),)),
        ],
    )(*operands)


def shards(anchor_mesh, stiffness, tissue, flow_blocks, confidence, flow_dest, flow_slot):
    flow = (
        flow_blocks.reshape(SECTIONS, TILES, 2, 2, 128).transpose(0, 1, 3, 2, 4).reshape(SECTIONS, 4 * TILES, 128)
    )
    dest = flow_dest.reshape(SECTIONS, TILES)

    def exchanged(buffer):
        buffer = buffer.reshape(TILES, LINES, 1, 128)
        arrived = lax.all_to_all(buffer, ("row", "col"), split_axis=0, concat_axis=0, tiled=True)
        return arrived.reshape(TILES * LINES, 128)

    stiffness = stiffness[None]
    arrived = exchanged(pack(GROUP, flow, confidence, dest, flow_slot, 56 << 20))
    pulled, top, bottom = land(GROUP, arrived, tissue, [anchor_mesh, stiffness])
    strips = ring([pulled, anchor_mesh, stiffness], top, bottom)
    return relax(GROUP, anchor_mesh, stiffness, pulled, strips)


def solution(mesh):
    placed = (
        P(None, "row", "col"),
        P("row", "col"),
        P(None, "row", "col"),
        P(None, ("row", "col"), None, None),
        P(None, ("row", "col"), None),
        P(None, ("row", "col"), None),
        P(None, ("row", "col")),
    )
    return jax.shard_map(
        shards, mesh=mesh, in_specs=placed, out_specs=P(None, None, "row", "col"), check_vma=False
    )
```

time: 1570 us -> 133 us (0.08); the launches traced: 1550 us -> 131 us
  starting transfers between devices: 662 us -> 16.8 us
  waiting for transfers between devices: 457 us -> 9.99 us
  local copies, waits for them, and re-layouts: 217 us -> 0.02 us
  other arithmetic: 210 us -> 0 us
  Pallas kernels: 0 us -> 54 us
  blocking collectives: 0 us -> 49.7 us
    ppermute x212 -> x6, starting transfers between devices: 597 us -> 16.8 us  [shifted(): return lax.ppermute(cells, axis, pairs)]
    ppermute x212 -> x6, waiting for transfers between devices: 426 us -> 9.99 us  [shifted(): return lax.ppermute(cells, axis, pairs)]
    slice x126 -> x0, local copies, waits for them, and re-layouts: 106 us -> none  [the longest x12 46.1 us: shards(): grid[:2] * mask]
    add x54 -> x0, other arithmetic: 86.6 us -> none  [the longest x48 77.6 us: relax(): return centre + damping_weight * (total / diagonal - centre)]
    concatenate x108 -> x0, other arithmetic: 78.6 us -> none  [the longest x106 75.7 us: with_halo(): jnp.concatenate([lax.ppermute(tail, axis, [(i, (i + 1) % count) for i in...]
    all_to_all x8 -> x0, starting transfers between devices: 65.3 us -> none  [the longest x4 32.7 us: shards(): lax.all_to_all(buffer.reshape(tiles, CAP, 3, buffer.shape[-1]), ('row', '...]
    pallas_call x0 -> x5, Pallas kernels: none -> 54 us  [the longest x1 36.5 us: relax(): call(lambda *refs: relax_kernel(group, *refs), 'relax', 96 << 20, jax.Sha...]
    all_to_all x0 -> x1, blocking collectives: none -> 49.7 us  [exchanged(): lax.all_to_all(buffer, ('row', 'col'), split_axis=0, concat_axis=0, tiled...]
  transfers between devices with their start and end apart: 220 -> 6, of which waited for: 156 -> 4; matrix products, arithmetic and copies ran while one was open for 8% -> 0% of each run, Pallas kernels for 0% -> 1%
where the time goes in v1:
time: 133 us; the launch traced here: 131 us
  Pallas kernels  54 us (41%)
  blocking collectives  49.7 us (37%)
  starting transfers between devices  16.8 us (13%)
  waiting for transfers between devices  9.99 us (8%)
    all_to_all x1, blocking collectives, exchanged(): lax.all_to_all(buffer, ('row', 'col'), split_axis=0, concat_axis=0, tiled...  49.7 us
    pallas_call x1, Pallas kernels, relax(): call(lambda *refs: relax_kernel(group, *refs), 'relax', 96 << 20, jax.Sha...  36.5 us
    ppermute x6, starting transfers between devices, shifted(): return lax.ppermute(cells, axis, pairs)  16.8 us
    pallas_call x1, Pallas kernels, land(): call(lambda *refs: land_kernel(group, *refs), 'land', 16 << 20, [jax.Shap...  11.5 us
    ppermute x6, waiting for transfers between devices, shifted(): return lax.ppermute(cells, axis, pairs)  9.99 us
    pallas_call x1, Pallas kernels, pack(): call(lambda *refs: pack_kernel(group, *refs), 'pack', 8 << 20, jax.ShapeD...  4.77 us
  transfers between devices with their start and end apart: 6, of which 4 were waited for; matrix products, arithmetic and copies ran while one was open for 0% of the time, Pallas kernels for 1%

profile of v1, /device:TPU:30, one launch (start us, length us, event | category | flops | bytes accessed | tf_op | source)
XLA Modules:
  0.0 130.8 jit_solution(3572148779896896775)
XLA Ops:
  0.0 4.8 %pack.1 = f32[6272,128]{1,0:T(8,128)} custom-call(f32[4,512,128]{2,1,0:T(8,128)} %bitcast.14, f32[4,128,256]{2,1,0:T(8,128)} %refs_1_.3, s32[4,128]{1,0:T(4,128)} %bitcast.15, s32[4,128]{1,0:T(4,128)} %refs_3_.1), custom_call_target="tpu_custom_call" | custom-call | bytes 8388608 | tf_op jit(solution)/shard_map/pack/pallas_call | solution.py:117
  4.8 0.0 copy-start
  4.8 0.0 copy-start.1
  4.8 0.0 copy-start.2
  4.8 49.7 %all_to_all.5 = f32[128,49,1,128]{3,2,1,0:T(1,128)S(1)} all-to-all(f32[128,49,1,128]{3,2,1,0:T(1,128)} %bitcast.13), channel_id=1, replica_groups=mesh['row'=16,'col'=8] {'row','col'}, dimensions={0} | all-to-all | bytes 6422528 | tf_op jit(solution)/shard_map/all_to_all | solution.py:538
  54.5 0.0 copy-done
  54.5 0.0 copy-done.1
  54.5 0.0 copy-done.2
  54.5 11.5 %land.1 = (f32[12,2,256,128]{3,2,1,0:T(8,128)S(1)}, f32[528,256]{1,0:T(8,128)S(1)}, f32[528,256]{1,0:T(8,128)S(1)}) custom-call(f32[6272,128]{1,0:T(8,128)S(1)} %bitcast.9, s32[4,256,256]{2,1,0:T(8,128)S(1)} %copy-done.2, f32[2,256,256]{2,1,0:T(8,128)S(1)} %copy-done, f32[1,256,256]{2,1,0:T(8,128)S(1)} %bitcast.10), custom_call_target="tpu_custom_call" | custom-call | bytes 16777216 | tf_op jit(solution)/shard_map/land/pallas_call | solution.py:207
  66.0 1.9 %collective-permute-start = (f32[528,256]{1,0:T(8,128)S(1)}, f32[528,256]{1,0:T(8,128)S(1)}, u32[]{:S(2)}, u32[]{:S(2)}) collective-permute-start(f32[528,256]{1,0:T(8,128)S(1)} %get-tuple-element.13), channel_id=1, source_target_pairs={{0,8},{8,16},{16,24},{24,32},{32,40},{40,48},{48,56},{56,64},{64,7... | collective-permute-start | bytes 1622024 | tf_op jit(solution)/shard_map/ppermute | solution.py:296
  67.9 6.0 %collective-permute-start.1 = (f32[528,256]{1,0:T(8,128)S(1)}, f32[528,256]{1,0:T(8,128)S(1)}, u32[]{:S(2)}, u32[]{:S(2)}) collective-permute-start(f32[528,256]{1,0:T(8,128)S(1)} %get-tuple-element.14), channel_id=1, source_target_pairs={{8,0},{16,8},{24,16},{32,24},{40,32},{48,40},{56,48},{64,56},{72,6... | collective-permute-start | bytes 1622024 | tf_op jit(solution)/shard_map/ppermute | solution.py:296
  74.0 0.9 columns.1
  74.9 1.9 %collective-permute-start.2 = (f32[9,128,128]{2,1,0:T(8,128)S(1)}, f32[9,128,128]{2,1,0:T(8,128)S(1)}, u32[]{:S(2)}, u32[]{:S(2)}) collective-permute-start(f32[9,128,128]{2,1,0:T(8,128)S(1)} %get-tuple-element.15), channel_id=1, source_target_pairs={{1,0},{2,1},{3,2},{4,3},{5,4},{6,5},{7,6},{9,8},{10,9},{11,10},{12... | collective-permute-start | bytes 1769480 | tf_op jit(solution)/shard_map/ppermute | solution.py:296
  76.8 2.4 %collective-permute-start.3 = (f32[9,128,128]{2,1,0:T(8,128)S(1)}, f32[9,128,128]{2,1,0:T(8,128)S(1)}, u32[]{:S(2)}, u32[]{:S(2)}) collective-permute-start(f32[9,128,128]{2,1,0:T(8,128)S(1)} %get-tuple-element.16), channel_id=1, source_target_pairs={{0,1},{1,2},{2,3},{3,4},{4,5},{5,6},{6,7},{8,9},{9,10},{10,11},{11... | collective-permute-start | bytes 1769480 | tf_op jit(solution)/shard_map/ppermute | solution.py:296
  79.3 4.2 %collective-permute-done.above_ref.refs_3_ = f32[528,256]{1,0:T(8,128)S(1)} collective-permute-done((f32[528,256]{1,0:T(8,128)S(1)}, f32[528,256]{1,0:T(8,128)S(1)}, u32[]{:S(2)}, u32[]{:S(2)}) %collective-permute-start) | collective-permute-done | bytes 540704 | tf_op jit(solution)/shard_map/ppermute | solution.py:296
  83.5 1.2 collective-permute-done.1.below_ref.refs_4_
  84.6 0.3 corners.1
  85.0 1.9 %collective-permute-start.4 = (f32[9,48,128]{2,1,0:T(8,128)S(1)}, f32[9,48,128]{2,1,0:T(8,128)S(1)}, u32[]{:S(2)}, u32[]{:S(2)}) collective-permute-start(f32[9,48,128]{2,1,0:T(8,128)S(1)} %get-tuple-element.17), channel_id=1, source_target_pairs={{1,0},{2,1},{3,2},{4,3},{5,4},{6,5},{7,6},{9,8},{10,9},{11,10},{12... | collective-permute-start | bytes 663560 | tf_op jit(solution)/shard_map/ppermute | solution.py:296
  86.9 2.6 %collective-permute-start.5 = (f32[9,48,128]{2,1,0:T(8,128)S(1)}, f32[9,48,128]{2,1,0:T(8,128)S(1)}, u32[]{:S(2)}, u32[]{:S(2)}) collective-permute-start(f32[9,48,128]{2,1,0:T(8,128)S(1)} %get-tuple-element.18), channel_id=1, source_target_pairs={{0,1},{1,2},{2,3},{3,4},{4,5},{5,6},{6,7},{8,9},{9,10},{10,11},{11... | collective-permute-start | bytes 663560 | tf_op jit(solution)/shard_map/ppermute | solution.py:296
  89.5 0.0 collective-permute-done.2.refs_5_
  89.5 0.0 collective-permute-done.3.refs_6_
  89.5 0.8 collective-permute-done.4.refs_7_
  90.3 3.8 %collective-permute-done.5.refs_8_ = f32[9,48,128]{2,1,0:T(8,128)S(1)} collective-permute-done((f32[9,48,128]{2,1,0:T(8,128)S(1)}, f32[9,48,128]{2,1,0:T(8,128)S(1)}, u32[]{:S(2)}, u32[]{:S(2)}) %collective-permute-start.5) | collective-permute-done | bytes 221216 | tf_op jit(solution)/shard_map/ppermute | solution.py:296
  94.1 36.5 %relax.1 = f32[4,2,256,256]{3,2,1,0:T(8,128)} custom-call(f32[2,256,256]{2,1,0:T(8,128)S(1)} %copy-done, f32[1,256,256]{2,1,0:T(8,128)S(1)} %bitcast.12, f32[12,2,256,128]{3,2,1,0:T(8,128)S(1)} %get-tuple-element.12.refs_0_.refs_2_, f32[528,256]{1,0:T(8,128)S(1)} %collective-permute-done.above_ref.refs_3_, ...), custom_call_target="tpu_custom_call" | custom-call | bytes 100663296 | tf_op jit(solution)/shard_map/relax/pallas_call | solution.py:506
Async XLA Ops:
  4.8 49.7 %copy-start = (f32[2,256,256]{2,1,0:T(8,128)S(1)}, f32[2,256,256]{2,1,0:T(8,128)}, u32[]{:S(2)}) copy-start(f32[2,256,256]{2,1,0:T(8,128)} %refs_0_.1) | copy-start | bytes 1572868
  4.8 49.7 %copy-start.1 = (f32[256,256]{1,0:T(8,128)S(1)}, f32[256,256]{1,0:T(8,128)}, u32[]{:S(2)}) copy-start(f32[256,256]{1,0:T(8,128)} %param.8) | copy-start | bytes 786436
  4.8 49.7 %copy-start.2 = (s32[4,256,256]{2,1,0:T(8,128)S(1)}, s32[4,256,256]{2,1,0:T(8,128)}, u32[]{:S(2)}) copy-start(s32[4,256,256]{2,1,0:T(8,128)} %refs_1_.4) | copy-start | bytes 3145732
  66.0 17.4 %collective-permute-start = (f32[528,256]{1,0:T(8,128)S(1)}, f32[528,256]{1,0:T(8,128)S(1)}, u32[]{:S(2)}, u32[]{:S(2)}) collective-permute-start(f32[528,256]{1,0:T(8,128)S(1)} %get-tuple-element.13), channel_id=1, source_target_pairs={{0,8},{8,16},{16,24},{24,32},{32,40},{40,48},{48,56},{56,64},{64,7... | collective-permute-start | bytes 1622024 | tf_op jit(solution)/shard_map/ppermute | solution.py:296
  67.9 16.7 %collective-permute-start.1 = (f32[528,256]{1,0:T(8,128)S(1)}, f32[528,256]{1,0:T(8,128)S(1)}, u32[]{:S(2)}, u32[]{:S(2)}) collective-permute-start(f32[528,256]{1,0:T(8,128)S(1)} %get-tuple-element.14), channel_id=1, source_target_pairs={{8,0},{16,8},{24,16},{32,24},{40,32},{48,40},{56,48},{64,56},{72,6... | collective-permute-start | bytes 1622024 | tf_op jit(solution)/shard_map/ppermute | solution.py:296
  74.9 14.6 %collective-permute-start.2 = (f32[9,128,128]{2,1,0:T(8,128)S(1)}, f32[9,128,128]{2,1,0:T(8,128)S(1)}, u32[]{:S(2)}, u32[]{:S(2)}) collective-permute-start(f32[9,128,128]{2,1,0:T(8,128)S(1)} %get-tuple-element.15), channel_id=1, source_target_pairs={{1,0},{2,1},{3,2},{4,3},{5,4},{6,5},{7,6},{9,8},{10,9},{11,10},{12... | collective-permute-start | bytes 1769480 | tf_op jit(solution)/shard_map/ppermute | solution.py:296
  76.8 12.7 %collective-permute-start.3 = (f32[9,128,128]{2,1,0:T(8,128)S(1)}, f32[9,128,128]{2,1,0:T(8,128)S(1)}, u32[]{:S(2)}, u32[]{:S(2)}) collective-permute-start(f32[9,128,128]{2,1,0:T(8,128)S(1)} %get-tuple-element.16), channel_id=1, source_target_pairs={{0,1},{1,2},{2,3},{3,4},{4,5},{5,6},{6,7},{8,9},{9,10},{10,11},{11... | collective-permute-start | bytes 1769480 | tf_op jit(solution)/shard_map/ppermute | solution.py:296
  85.0 5.4 %collective-permute-start.4 = (f32[9,48,128]{2,1,0:T(8,128)S(1)}, f32[9,48,128]{2,1,0:T(8,128)S(1)}, u32[]{:S(2)}, u32[]{:S(2)}) collective-permute-start(f32[9,48,128]{2,1,0:T(8,128)S(1)} %get-tuple-element.17), channel_id=1, source_target_pairs={{1,0},{2,1},{3,2},{4,3},{5,4},{6,5},{7,6},{9,8},{10,9},{11,10},{12... | collective-permute-start | bytes 663560 | tf_op jit(solution)/shard_map/ppermute | solution.py:296
  86.9 7.3 %collective-permute-start.5 = (f32[9,48,128]{2,1,0:T(8,128)S(1)}, f32[9,48,128]{2,1,0:T(8,128)S(1)}, u32[]{:S(2)}, u32[]{:S(2)}) collective-permute-start(f32[9,48,128]{2,1,0:T(8,128)S(1)} %get-tuple-element.18), channel_id=1, source_target_pairs={{0,1},{1,2},{2,3},{3,4},{4,5},{5,6},{6,7},{8,9},{9,10},{10,11},{11... | collective-permute-start | bytes 663560 | tf_op jit(solution)/shard_map/ppermute | solution.py:296
